TPU v7x, 32 devices: a whole 2x2x4 slice. The times are simulated.
32 devices in a mesh: group: 2 (over x), row: 16 (over z, y, core).
Axes of the slice: x: 2, y: 2, z: 4, core: 2. Of those that a mesh axis runs over, the one named last changes fastest.
Arguments:
- base_currents: bfloat16 [32768, 1024], P(('group', 'row')), parts along dimension 0, may hold values from -6 to 6
- term_rows: bfloat16 [8192, 1024], P(('group', 'row')), parts along dimension 0, may hold values from -12 to 12
- term_owner: int32 [8192, 1], P(('group', 'row')), parts along dimension 0, may hold values from 0 to 15; in each aligned block of 256 rows (0 to 255, 256 to 511, ...) at most 32 rows name the same one
- term_slot: int32 [8192, 1], P(('group', 'row')), parts along dimension 0, may hold values from 0 to 1023
- inductance: bfloat16 [64, 20, 256, 256], P('row'), may hold values from -0.078125 to 0.078125
- block_cols: int32 [64, 20], P('row'), may hold values from 0 to 63, as said below
Outputs:
- flux: bfloat16 [32768, 1024], P(('group', 'row')), parts along dimension 0
There are 2 independent parts, one for each index of `group`. A program takes and returns all parts, laid end to end along the dimension named above; an argument that names none is the same for every part. Nothing has to cross between parts.
Inputs may be any that keep to these rules, and one draw needn't show every extreme that they name: `block_cols`: the block rows of device i (block rows i * 4 to i * 4 + 3) list only block columns of devices i - 2 to i + 2; every block row lists a column of device max(i - 2, 0) and one of device min(i + 2, the last device). Columns may repeat. `term_owner`: among the 256 terminal rows of one device, at most 32 name the same owner, and that many is reached.
All inputs are finite; a program needn't handle non-finite values.
Results may differ from a plain program's by a relative error of at most 0.0046.
Values may be sent and summed in bfloat16 or wider, within the bound.
A program may use at most 128 MiB of HBM per device.

v0:
```python
import jax
import jax.numpy as jnp
from jax import lax
from jax.sharding import PartitionSpec as P

HALO = 2


def shifted(value, axis, by):
    size = lax.axis_size(axis)
    pairs = [(i, i + by) for i in range(size) if 0 <= i + by < size]
    return lax.ppermute(value, axis, pairs)


def shards(base_currents, term_rows, term_owner, term_slot, inductance, block_cols):
    devices = lax.axis_size("row")
    own_index = lax.axis_index("row")
    seg_dev, width = base_currents.shape
    capacity = max(2, 2 * term_rows.shape[0] // devices)
    owner_ids = term_owner[:, 0]
    target = term_slot[:, 0]
    peer_ids = jnp.arange(devices, dtype=jnp.int32)
    matches = (owner_ids[:, None] == peer_ids[None, :]).astype(jnp.int32)
    earlier = jnp.cumsum(matches, axis=0) - matches
    order_in = jnp.sum(earlier * matches, axis=1)
    position = owner_ids * capacity + order_in
    slot_ids = jnp.arange(devices * capacity, dtype=jnp.int32)
    picker = slot_ids[:, None] == position[None, :]
    outgoing = jnp.dot(picker.astype(jnp.bfloat16), term_rows, preferred_element_type=jnp.float32)
    outgoing = outgoing.astype(jnp.bfloat16).reshape(devices, capacity, width)
    slot_tags = jnp.sum(jnp.where(picker, target[None, :] + 1, 0), axis=1)
    slot_tags = slot_tags.reshape(devices, capacity)
    arrived, arrived_tags = (
        lax.all_to_all(outgoing, "row", split_axis=0, concat_axis=0, tiled=True),
        lax.all_to_all(slot_tags, "row", split_axis=0, concat_axis=0, tiled=True),
    )
    seg_ids = jnp.arange(seg_dev, dtype=jnp.int32)
    landing = (arrived_tags.reshape(-1)[None, :] - 1 == seg_ids[:, None]).astype(jnp.bfloat16)
    injected = jnp.dot(landing, arrived.reshape(-1, width), preferred_element_type=jnp.float32)
    currents = (base_currents.astype(jnp.float32) + injected).astype(jnp.bfloat16)
    below = []
    above = []
    offsets = list(range(1, HALO + 1)) + [-step for step in range(1, HALO + 1)]
    for offset in offsets:
        moved = shifted(currents, "row", offset)
        if offset > 0:
            below.append(moved)
        else:
            above.append(moved)
    window = jnp.concatenate(below[::-1] + [currents] + above, axis=0)
    rows_dev = inductance.shape[0]
    block = inductance.shape[2]
    window_blocks = window.reshape(-1, block, width)
    first_block = (own_index - HALO) * rows_dev
    results = []
    for block_row in range(rows_dev):
        local_cols = block_cols[block_row] - first_block
        picked = window_blocks[local_cols]
        linked = jnp.einsum(
            "kab,kbw->aw", inductance[block_row], picked, preferred_element_type=jnp.float32
        )
        results.append(linked)
    return jnp.concatenate(results, axis=0).astype(jnp.bfloat16)


def solution(mesh):
    placed = (
        P(("group", "row"), None),
        P(("group", "row"), None),
        P(("group", "row"), None),
        P(("group", "row"), None),
        P("row", None, None, None),
        P("row", None),
    )
    return jax.shard_map(
        shards, mesh=mesh, in_specs=placed, out_specs=P(("group", "row"), None), check_vma=False
    )
```

profile of v0, /device:TPU:12, one launch (start us, length us, event | category | flops | bytes accessed | tf_op | source)
XLA Modules:
  0.0 267.3 jit_solution(7701543596068987871)
XLA Ops:
  0.0 0.0 copy-start
  0.0 0.0 copy-start.4
  0.0 0.7 fusion.53
  0.7 0.6 reduce-window.6
  1.3 0.2 slice_reduce_fusion
  1.5 0.8 fusion.52
  2.3 0.7 multiply_add_fusion
  3.0 0.7 broadcast_add_fusion
  3.7 0.1 select_reduce_fusion
  3.8 0.7 all_to_all.9
  4.5 6.2 %all-to-all-start = ((s32[16,1,32]{2,1,0:T(1,128)}), s32[16,1,32]{2,1,0:T(1,128)S(1)}, u32[]{:S(2)}, u32[]{:S(2)}) async-start(s32[16,1,32]{2,1,0:T(1,128)} %all_to_all.9), calls=%async_computation | async-start | bytes 16384 | tf_op jit(solution)/shard_map/all_to_all | solution.py:35
  10.8 0.0 copy-done
  10.8 1.4 convolution_convert_fusion
  12.2 2.7 all-to-all-done
  14.9 5.9 %all-to-all-start.1 = ((bf16[16,32,1024]{2,1,0:T(8,128)(2,1)}), bf16[16,32,1024]{2,1,0:T(8,128)(2,1)S(1)}, u32[]{:S(2)}, u32[]{:S(2)}) async-start(bf16[16,32,1024]{2,1,0:T(8,128)(2,1)} %bitcast.4), calls=%async_computation.1 | async-start | bytes 2097152 | tf_op jit(solution)/shard_map/all_to_all | solution.py:34
  20.8 0.1 sub.72
  20.9 24.6 %all-to-all-done.1 = bf16[16,32,1024]{2,1,0:T(8,128)(2,1)S(1)} async-done(((bf16[16,32,1024]{2,1,0:T(8,128)(2,1)}), bf16[16,32,1024]{2,1,0:T(8,128)(2,1)S(1)}, u32[]{:S(2)}, u32[]{:S(2)}) %all-to-all-start.1) | async-done | bytes 1048608 | tf_op jit(solution)/shard_map/all_to_all | solution.py:34
  45.5 0.0 copy-start.3
  45.5 1.0 copy-done.3
  46.5 3.2 %add_convert_fusion = bf16[1024,1024]{1,0:T(8,128)(2,1)S(1)} fusion(bf16[1024,1024]{1,0:T(8,128)(2,1)} %param.6, bf16[512,1024]{1,0:T(8,128)(2,1)} %bitcast.115, s32[512]{0:T(512)S(1)} %sub.72), kind=kOutput, calls=%fused_computation.4 | convolution fusion | flops 1077411840 | bytes 5244928 | tf_op jit(solution)/shard_map/dot_general | solution.py:39
  49.7 3.8 %collective-permute-start = (bf16[1024,1024]{1,0:T(8,128)(2,1)S(1)}, bf16[1024,1024]{1,0:T(8,128)(2,1)}, u32[]{:S(2)}, u32[]{:S(2)}) collective-permute-start(bf16[1024,1024]{1,0:T(8,128)(2,1)S(1)} %add_convert_fusion), channel_id=1, source_target_pairs={{0,2},{1,3},{2,4},{3,5},{4,6},{5,7},{6,8},{7,9},{8,10},{9,11},{10,... | collective-permute-start | bytes 6291464 | tf_op jit(solution)/shard_map/ppermute | solution.py:12
  53.5 1.9 collective-permute-start.1
  55.4 3.6 %collective-permute-start.2 = (bf16[1024,1024]{1,0:T(8,128)(2,1)S(1)}, bf16[1024,1024]{1,0:T(8,128)(2,1)}, u32[]{:S(2)}, u32[]{:S(2)}) collective-permute-start(bf16[1024,1024]{1,0:T(8,128)(2,1)S(1)} %add_convert_fusion), channel_id=1, source_target_pairs={{1,0},{2,1},{3,2},{4,3},{5,4},{6,5},{7,6},{8,7},{9,8},{10,9},{11,1... | collective-permute-start | bytes 6291464 | tf_op jit(solution)/shard_map/ppermute | solution.py:12
  59.1 2.9 %collective-permute-start.3 = (bf16[1024,1024]{1,0:T(8,128)(2,1)S(1)}, bf16[1024,1024]{1,0:T(8,128)(2,1)}, u32[]{:S(2)}, u32[]{:S(2)}) collective-permute-start(bf16[1024,1024]{1,0:T(8,128)(2,1)S(1)} %add_convert_fusion), channel_id=1, source_target_pairs={{2,0},{3,1},{4,2},{5,3},{6,4},{7,5},{8,6},{9,7},{10,8},{11,9},{12,... | collective-permute-start | bytes 6291464 | tf_op jit(solution)/shard_map/ppermute | solution.py:12
  62.0 0.0 copy-done.4
  62.1 105.5 %collective-permute-done = bf16[1024,1024]{1,0:T(8,128)(2,1)} collective-permute-done((bf16[1024,1024]{1,0:T(8,128)(2,1)S(1)}, bf16[1024,1024]{1,0:T(8,128)(2,1)}, u32[]{:S(2)}, u32[]{:S(2)}) %collective-permute-start) | collective-permute-done | bytes 2097184 | tf_op jit(solution)/shard_map/ppermute | solution.py:12
  167.5 3.1 %constant_dynamic-update-slice_fusion.4 = bf16[5120,1024]{1,0:T(8,128)(2,1)} fusion(bf16[1024,1024]{1,0:T(8,128)(2,1)} %collective-permute-done), kind=kLoop, calls=%fused_computation.49 | loop fusion | bytes 4194304
  170.6 18.7 %collective-permute-done.1 = bf16[1024,1024]{1,0:T(8,128)(2,1)} collective-permute-done((bf16[1024,1024]{1,0:T(8,128)(2,1)S(1)}, bf16[1024,1024]{1,0:T(8,128)(2,1)}, u32[]{:S(2)}, u32[]{:S(2)}) %collective-permute-start.1) | collective-permute-done | bytes 2097184 | tf_op jit(solution)/shard_map/ppermute | solution.py:12
  189.4 3.1 %constant_dynamic-update-slice_fusion.3 = bf16[5120,1024]{1,0:T(8,128)(2,1)} fusion(bf16[5120,1024]{1,0:T(8,128)(2,1)} %constant_dynamic-update-slice_fusion.4, bf16[1024,1024]{1,0:T(8,128)(2,1)} %collective-permute-done.1), kind=kLoop, calls=%fused_computation.48 | loop fusion | bytes 4194304
  192.4 1.5 constant_dynamic-update-slice_fusion.2
  193.9 0.0 collective-permute-done.2
  193.9 3.1 %constant_dynamic-update-slice_fusion.1 = bf16[5120,1024]{1,0:T(8,128)(2,1)} fusion(bf16[5120,1024]{1,0:T(8,128)(2,1)} %constant_dynamic-update-slice_fusion.2, bf16[1024,1024]{1,0:T(8,128)(2,1)} %collective-permute-done.2), kind=kLoop, calls=%fused_computation.46 | loop fusion | bytes 4194304
  197.1 0.0 collective-permute-done.3
  197.1 3.2 %constant_dynamic-update-slice_fusion = bf16[5120,1024]{1,0:T(8,128)(2,1)} fusion(bf16[5120,1024]{1,0:T(8,128)(2,1)} %constant_dynamic-update-slice_fusion.1, bf16[1024,1024]{1,0:T(8,128)(2,1)} %collective-permute-done.3), kind=kLoop, calls=%fused_computation.45 | loop fusion | bytes 4194304 | tf_op jit(solution)/shard_map/concatenate | solution.py:50
  200.2 9.7 %gather_fusion = bf16[20,256,1024]{2,1,0:T(8,128)(2,1)} fusion(bf16[20,256,1024]{2,1,0:T(8,128)(2,1)} %bitcast.6, s32[1024]{0:T(1024)S(1)} %get-tuple-element.12), kind=kCustom, calls=%fused_computation | custom fusion | bytes 20971600 | tf_op jit(solution)/shard_map/gather | solution.py:58
  209.9 9.4 %gather_fusion.1 = bf16[20,256,1024]{2,1,0:T(8,128)(2,1)} fusion(bf16[20,256,1024]{2,1,0:T(8,128)(2,1)} %bitcast.6, s32[1024]{0:T(1024)S(1)} %get-tuple-element.11), kind=kCustom, calls=%fused_computation.1 | custom fusion | bytes 20971600 | tf_op jit(solution)/shard_map/gather | solution.py:58
  219.2 0.0 copy-start.2
  219.2 7.8 %fusion.36 = bf16[256,1024]{1,0:T(8,128)(2,1)S(1)} fusion(bf16[20,256,1024]{2,1,0:T(8,128)(2,1)} %gather_fusion, bf16[4,20,256,256]{3,2,1,0:T(8,128)(2,1)} %param.10), kind=kOutput, calls=%fused_computation.28 | convolution fusion | flops 2684616704 | bytes 13631488 | tf_op jit(solution)/shard_map/kab,kbw->aw/dot_general | solution.py:59
  227.0 0.0 copy-done.2
  227.0 4.7 %fusion.39 = bf16[256,1024]{1,0:T(8,128)(2,1)S(1)} fusion(bf16[20,256,1024]{2,1,0:T(8,128)(2,1)S(1)} %copy-done.2, bf16[4,20,256,256]{3,2,1,0:T(8,128)(2,1)} %param.10), kind=kOutput, calls=%fused_computation.29 | convolution fusion | flops 2684616704 | bytes 13631488 | tf_op jit(solution)/shard_map/kab,kbw->aw/dot_general | solution.py:59
  231.7 9.4 %gather_fusion.2 = bf16[20,256,1024]{2,1,0:T(8,128)(2,1)} fusion(bf16[20,256,1024]{2,1,0:T(8,128)(2,1)} %bitcast.6, s32[1024]{0:T(1024)S(1)} %get-tuple-element.10), kind=kCustom, calls=%fused_computation.2 | custom fusion | bytes 20971600 | tf_op jit(solution)/shard_map/gather | solution.py:58
  241.1 7.6 %fusion.42 = bf16[256,1024]{1,0:T(8,128)(2,1)S(1)} fusion(bf16[20,256,1024]{2,1,0:T(8,128)(2,1)} %gather_fusion.2, bf16[4,20,256,256]{3,2,1,0:T(8,128)(2,1)} %param.10), kind=kOutput, calls=%fused_computation.30 | convolution fusion | flops 2684616704 | bytes 13631488 | tf_op jit(solution)/shard_map/kab,kbw->aw/dot_general | solution.py:59
  248.7 0.0 copy-start.1
  248.7 9.4 %gather_fusion.3 = bf16[20,256,1024]{2,1,0:T(8,128)(2,1)} fusion(bf16[20,256,1024]{2,1,0:T(8,128)(2,1)} %bitcast.6, s32[1024]{0:T(1024)S(1)} %get-tuple-element.9), kind=kCustom, calls=%fused_computation.3 | custom fusion | bytes 20971600 | tf_op jit(solution)/shard_map/gather | solution.py:58
  258.2 7.6 %fusion.45 = bf16[256,1024]{1,0:T(8,128)(2,1)S(1)} fusion(bf16[20,256,1024]{2,1,0:T(8,128)(2,1)} %gather_fusion.3, bf16[4,20,256,256]{3,2,1,0:T(8,128)(2,1)} %param.10), kind=kOutput, calls=%fused_computation.31 | convolution fusion | flops 2684616704 | bytes 13631488 | tf_op jit(solution)/shard_map/kab,kbw->aw/dot_general | solution.py:59
  265.8 1.5 pad_maximum_fusion
  267.3 0.0 copy-done.1
  (6 shorter events, 0.1 us)
Async XLA Ops:
  0.0 10.8 %copy-start = (bf16[256,1024]{1,0:T(8,128)(2,1)S(1)}, bf16[256,1024]{1,0:T(8,128)(2,1)}, u32[]{:S(2)}) copy-start(bf16[256,1024]{1,0:T(8,128)(2,1)} %param.7) | copy-start | bytes 1572868
  0.0 62.0 %copy-start.4 = (s32[4,20]{1,0:T(4,128)S(1)}, s32[4,20]{1,0:T(4,128)}, u32[]{:S(2)}) copy-start(s32[4,20]{1,0:T(4,128)} %param.11) | copy-start | bytes 964
  4.5 10.3 %all-to-all-start = ((s32[16,1,32]{2,1,0:T(1,128)}), s32[16,1,32]{2,1,0:T(1,128)S(1)}, u32[]{:S(2)}, u32[]{:S(2)}) async-start(s32[16,1,32]{2,1,0:T(1,128)} %all_to_all.9), calls=%async_computation | async-start | bytes 16384 | tf_op jit(solution)/shard_map/all_to_all | solution.py:35
  14.9 30.6 %all-to-all-start.1 = ((bf16[16,32,1024]{2,1,0:T(8,128)(2,1)}), bf16[16,32,1024]{2,1,0:T(8,128)(2,1)S(1)}, u32[]{:S(2)}, u32[]{:S(2)}) async-start(bf16[16,32,1024]{2,1,0:T(8,128)(2,1)} %bitcast.4), calls=%async_computation.1 | async-start | bytes 2097152 | tf_op jit(solution)/shard_map/all_to_all | solution.py:34
  45.5 1.0 copy-start.3
  49.7 117.9 %collective-permute-start = (bf16[1024,1024]{1,0:T(8,128)(2,1)S(1)}, bf16[1024,1024]{1,0:T(8,128)(2,1)}, u32[]{:S(2)}, u32[]{:S(2)}) collective-permute-start(bf16[1024,1024]{1,0:T(8,128)(2,1)S(1)} %add_convert_fusion), channel_id=1, source_target_pairs={{0,2},{1,3},{2,4},{3,5},{4,6},{5,7},{6,8},{7,9},{8,10},{9,11},{10,... | collective-permute-start | bytes 6291464 | tf_op jit(solution)/shard_map/ppermute | solution.py:12
  53.5 135.9 %collective-permute-start.1 = (bf16[1024,1024]{1,0:T(8,128)(2,1)S(1)}, bf16[1024,1024]{1,0:T(8,128)(2,1)}, u32[]{:S(2)}, u32[]{:S(2)}) collective-permute-start(bf16[1024,1024]{1,0:T(8,128)(2,1)S(1)} %add_convert_fusion), channel_id=1, source_target_pairs={{0,1},{1,2},{2,3},{3,4},{4,5},{5,6},{6,7},{7,8},{8,9},{9,10},{10,1... | collective-permute-start | bytes 6291464 | tf_op jit(solution)/shard_map/ppermute | solution.py:12
  55.4 138.5 %collective-permute-start.2 = (bf16[1024,1024]{1,0:T(8,128)(2,1)S(1)}, bf16[1024,1024]{1,0:T(8,128)(2,1)}, u32[]{:S(2)}, u32[]{:S(2)}) collective-permute-start(bf16[1024,1024]{1,0:T(8,128)(2,1)S(1)} %add_convert_fusion), channel_id=1, source_target_pairs={{1,0},{2,1},{3,2},{4,3},{5,4},{6,5},{7,6},{8,7},{9,8},{10,9},{11,1... | collective-permute-start | bytes 6291464 | tf_op jit(solution)/shard_map/ppermute | solution.py:12
  59.1 138.0 %collective-permute-start.3 = (bf16[1024,1024]{1,0:T(8,128)(2,1)S(1)}, bf16[1024,1024]{1,0:T(8,128)(2,1)}, u32[]{:S(2)}, u32[]{:S(2)}) collective-permute-start(bf16[1024,1024]{1,0:T(8,128)(2,1)S(1)} %add_convert_fusion), channel_id=1, source_target_pairs={{2,0},{3,1},{4,2},{5,3},{6,4},{7,5},{8,6},{9,7},{10,8},{11,9},{12,... | collective-permute-start | bytes 6291464 | tf_op jit(solution)/shard_map/ppermute | solution.py:12
  219.2 7.8 %copy-start.2 = (bf16[20,256,1024]{2,1,0:T(8,128)(2,1)S(1)}, bf16[20,256,1024]{2,1,0:T(8,128)(2,1)}, u32[]{:S(2)}) copy-start(bf16[20,256,1024]{2,1,0:T(8,128)(2,1)} %gather_fusion.1) | copy-start | bytes 31457284
  248.7 18.6 %copy-start.1 = (bf16[256,1024]{1,0:T(8,128)(2,1)S(1)}, bf16[256,1024]{1,0:T(8,128)(2,1)}, u32[]{:S(2)}) copy-start(bf16[256,1024]{1,0:T(8,128)(2,1)} %param.7) | copy-start | bytes 1572868
where the time goes:
time: 268 us; the launch traced here: 267 us
  waiting for transfers between devices  152 us (57%)
  local copies, waits for them, and re-layouts  53.7 us (20%)
  matrix products  32.4 us (12%)
  starting transfers between devices  24.4 us (9%)
  other arithmetic  5.17 us (2%)
    ppermute x4, waiting for transfers between devices, shifted(): return lax.ppermute(value, axis, pairs)  124 us
    gather x4, local copies, waits for them, and re-layouts, shards(): picked = window_blocks[local_cols]  37.8 us
    dot_general x4, matrix products, shards(): jnp.einsum('kab,kbw->aw', inductance[block_row], picked, preferred_elemen...  27.7 us
    all_to_all x1, waiting for transfers between devices, shards(): lax.all_to_all(outgoing, 'row', split_axis=0, concat_axis=0, tiled=True)  24.6 us
    ppermute x4, starting transfers between devices, shifted(): return lax.ppermute(value, axis, pairs)  12.3 us
    unnamed x14, local copies, waits for them, and re-layouts  11.8 us
    all_to_all x1, starting transfers between devices, shards(): lax.all_to_all(slot_tags, 'row', split_axis=0, concat_axis=0, tiled=True)  6.24 us
    all_to_all x1, starting transfers between devices, shards(): lax.all_to_all(outgoing, 'row', split_axis=0, concat_axis=0, tiled=True)  5.89 us
  transfers between devices with their start and end apart: 6, of which 4 were waited for; matrix products, arithmetic and copies ran while one was open for 5% of the time, Pallas kernels for 0%

commit v1 on v0

v1 whole, which is shorter than its diff:
```python
import functools

import jax
import jax.numpy as jnp
from jax import lax
from jax.experimental import pallas as pl
from jax.experimental.pallas import tpu as pltpu
from jax.sharding import PartitionSpec as P

CHUNKS = 4
LANES = 128
HALO = 2
MESH = pl.DeviceIdType.MESH
F32 = jnp.float32
BF16 = jnp.bfloat16
TO_Y, TO_Z, TO_CORE, TO_RELAY = range(4)


def kernel(n, cap, cols_ref, owner_ref, slot_ref, terms_hbm, base_hbm, blocks_hbm, out_hbm, *scratch):
    windows, scratch = scratch[:CHUNKS], scratch[CHUNKS:]
    outgoing, scratch = scratch[:CHUNKS], scratch[CHUNKS:]
    arrived, scratch = scratch[:CHUNKS], scratch[CHUNKS:]
    results, scratch = scratch[:CHUNKS], scratch[CHUNKS:]
    (terms, base, blocks, landing, tags_out, tags_in,
     load_sem, own_sem, store_sem, a2a_send, a2a_recv, tag_send, tag_recv, halo_send, halo_recv) = scratch
    me = lax.axis_index("row")
    count = terms.shape[0]
    seg_dev = base.shape[0]
    rows_dev, stored, block, _ = blocks.shape
    wide = windows[0].shape[2]
    sign_c = 1 - 2 * (me % 2)
    sign_y = 1 - 2 * ((me // 2) % 2)
    z_to, z_from = me + 4 * sign_y, me - 4 * sign_y
    z_sends = jnp.logical_and(z_to >= 0, z_to < n)
    z_comes = jnp.logical_and(z_from >= 0, z_from < n)

    load_terms = pltpu.make_async_copy(terms_hbm, terms, load_sem.at[0])
    load_base = pltpu.make_async_copy(base_hbm, base, load_sem.at[1])
    load_blocks = pltpu.make_async_copy(blocks_hbm, blocks, load_sem.at[2])
    load_terms.start()
    load_base.start()
    load_blocks.start()

    barrier = pltpu.get_barrier_semaphore()

    @pl.loop(1, n)
    def _(step):
        pl.semaphore_signal(barrier, inc=1, device_id={"row": (me + step) % n}, device_id_type=MESH)

    owner = owner_ref[...]
    matches = (lax.broadcasted_iota(jnp.int32, (n, count), 0) == owner).astype(F32)
    before = lax.broadcasted_iota(jnp.int32, (count, count), 0) < lax.broadcasted_iota(jnp.int32, (count, count), 1)
    earlier = jnp.dot(matches.astype(BF16), before.astype(F32).astype(BF16), preferred_element_type=F32)
    order_in = jnp.sum(earlier * matches, axis=0, keepdims=True).astype(jnp.int32)
    position = owner * cap + order_in
    picker = (lax.broadcasted_iota(jnp.int32, (n * cap, count), 0) == position).astype(F32).astype(BF16)
    per_row = LANES // cap
    lane_of = order_in + (me % per_row) * cap
    lanes = (lax.broadcasted_iota(jnp.int32, (LANES, count), 0) == lane_of).astype(F32).astype(BF16)
    tag = slot_ref[...] + 1
    high = (tag // 32).astype(F32)
    low = (tag % 32).astype(F32)
    over_rows = (((1,), (1,)), ((), ()))
    tags = 32.0 * lax.dot_general((matches * high).astype(BF16), lanes, over_rows, preferred_element_type=F32)
    tags = tags + lax.dot_general((matches * low).astype(BF16), lanes, over_rows, preferred_element_type=F32)
    tags = tags.astype(jnp.int32)
    for peer in range(n):
        tags_out[peer] = jnp.broadcast_to(tags[peer:peer + 1], tags_out.shape[1:])

    def tag_copy(peer, source):
        return pltpu.make_async_remote_copy(
            src_ref=tags_out.at[peer], dst_ref=tags_in.at[source], send_sem=tag_send.at[peer],
            recv_sem=tag_recv.at[source], device_id={"row": peer}, device_id_type=MESH)

    def row_copy(j, peer, source):
        return pltpu.make_async_remote_copy(
            src_ref=outgoing[j].at[peer], dst_ref=arrived[j].at[source], send_sem=a2a_send.at[j, peer],
            recv_sem=a2a_recv.at[j, source], device_id={"row": peer}, device_id_type=MESH)

    load_terms.wait()
    pl.semaphore_wait(barrier, n - 1)

    @pl.loop(1, n)
    def _(step):
        tag_copy((me + step) % n, me).start()

    own_tags = pltpu.make_async_copy(tags_out.at[me], tags_in.at[me], own_sem.at[CHUNKS])
    own_tags.start()
    own_rows = []
    for j in range(CHUNKS):
        sent = jnp.dot(picker, terms[:, j * wide:(j + 1) * wide], preferred_element_type=F32)
        outgoing[j][...] = sent.astype(BF16).reshape(outgoing[j].shape)

        @pl.loop(1, n)
        def _(step):
            row_copy(j, (me + step) % n, me).start()

        own_rows.append(pltpu.make_async_copy(outgoing[j].at[me], arrived[j].at[me], own_sem.at[j]))
        own_rows[-1].start()

    @pl.loop(1, n)
    def _(step):
        source = (me + step) % n
        tag_copy(source, source).wait_recv()

    own_tags.wait()
    packed = []
    for first in range(0, n, per_row):
        total = tags_in[first][0:1]
        for source in range(first + 1, min(first + per_row, n)):
            total = total + tags_in[source][0:1]
        packed.append(total)
    arrived_tags = jnp.concatenate(packed, axis=1) - 1
    tall = seg_dev // 4
    for part in range(4):
        seg_ids = lax.broadcasted_iota(jnp.int32, (tall, n * cap), 0) + part * tall
        landing[part * tall:(part + 1) * tall] = (seg_ids == arrived_tags).astype(F32).astype(BF16)
    load_base.wait()

    def halo_copy(kind, j, from_slot, to_slot, peer):
        return pltpu.make_async_remote_copy(
            src_ref=windows[j].at[pl.ds(rows_dev * from_slot, rows_dev)],
            dst_ref=windows[j].at[pl.ds(rows_dev * to_slot, rows_dev)],
            send_sem=halo_send.at[kind, j], recv_sem=halo_recv.at[kind, j],
            device_id={"row": peer}, device_id_type=MESH)

    def y_send(j):
        return halo_copy(TO_Y, j, HALO, HALO - 2 * sign_y, me + 2 * sign_y)

    def core_send(j):
        return halo_copy(TO_CORE, j, HALO, HALO - sign_c, me + sign_c)

    def z_send(j):
        return halo_copy(TO_Z, j, HALO + 2 * sign_y, HALO - 2 * sign_y, z_to)

    def relay_send(j):
        return halo_copy(TO_RELAY, j, HALO + 2 * sign_c, HALO + sign_c, me + sign_c)

    def wait_for(kind, j, slot, peer):
        halo_copy(kind, j, slot, slot, peer).wait_recv()

    def own(j):
        @pl.loop(1, n)
        def _(step):
            source = (me + step) % n
            row_copy(j, source, source).wait_recv()

        own_rows[j].wait()
        rows = arrived[j][...].reshape(n * cap, wide)
        for part in range(seg_dev // block):
            place = slice(part * block, (part + 1) * block)
            injected = jnp.dot(landing[place], rows, preferred_element_type=F32)
            before_it = base[place, j * wide:(j + 1) * wide].astype(F32)
            windows[j][HALO * rows_dev + part] = (before_it + injected).astype(BF16)
        y_send(j).start()
        core_send(j).start()

    def y_arrives(j):
        wait_for(TO_Y, j, HALO + 2 * sign_y, me + 2 * sign_y)

        @pl.when(z_sends)
        def _():
            z_send(j).start()

        @pl.when(sign_y == sign_c)
        def _():
            relay_send(j).start()

    def z_arrives(j):
        @pl.when(z_comes)
        def _():
            wait_for(TO_Z, j, HALO - 2 * sign_y, me + 2 * sign_y)

        @pl.when(jnp.logical_and(z_comes, sign_y != sign_c))
        def _():
            relay_send(j).start()

    relay_sends = jnp.logical_or(sign_y == sign_c, z_comes)
    relay_comes = jnp.logical_or(sign_y != sign_c, z_comes)
    first_block = (me - HALO) * rows_dev

    def compute(j):
        wait_for(TO_CORE, j, HALO + sign_c, me + sign_c)

        @pl.when(relay_comes)
        def _():
            wait_for(TO_RELAY, j, HALO - sign_c, me + sign_c)

        @pl.loop(0, rows_dev)
        def _(r):
            total = jnp.zeros((block, wide), F32)
            for k in range(stored):
                place = jnp.clip(cols_ref[r, k] - first_block, 0, windows[j].shape[0] - 1)
                picked = windows[j][place]
                total = total + jnp.dot(blocks[r, k], picked, preferred_element_type=F32)
            results[j][pl.ds(pl.multiple_of(r * block, block), block)] = total.astype(BF16)

        store(j).start()

    def store(j):
        return pltpu.make_async_copy(results[j], out_hbm.at[:, pl.ds(j * wide, wide)], store_sem.at[j])

    own(0)
    own(1)
    for j in range(CHUNKS):
        y_arrives(j)
        if j + 2 < CHUNKS:
            own(j + 2)
        if j == 0:
            load_blocks.wait()
        else:
            z_arrives(j - 1)
            compute(j - 1)
    z_arrives(CHUNKS - 1)
    compute(CHUNKS - 1)

    @pl.loop(1, n)
    def _(step):
        peer = (me + step) % n
        tag_copy(peer, me).wait_send()
        for j in range(CHUNKS):
            row_copy(j, peer, me).wait_send()

    for j in range(CHUNKS):
        y_send(j).wait_send()
        core_send(j).wait_send()

        @pl.when(z_sends)
        def _():
            z_send(j).wait_send()

        @pl.when(relay_sends)
        def _():
            relay_send(j).wait_send()

        store(j).wait()


def shards(base_currents, term_rows, term_owner, term_slot, inductance, block_cols):
    n = lax.axis_size("row")
    seg_dev, width = base_currents.shape
    count = term_rows.shape[0]
    rows_dev, stored, block, _ = inductance.shape
    cap = max(16, 2 * count // n)
    wide = width // CHUNKS
    span = (2 * HALO + 1) * rows_dev
    vmem = pl.BlockSpec(memory_space=pltpu.VMEM)
    smem = pl.BlockSpec(memory_space=pltpu.SMEM)
    hbm = pl.BlockSpec(memory_space=pl.ANY)
    dma = pltpu.SemaphoreType.DMA
    return pl.pallas_call(
        functools.partial(kernel, n, cap),
        out_shape=jax.ShapeDtypeStruct((seg_dev, width), BF16),
        in_specs=[smem, vmem, vmem, hbm, hbm, hbm],
        out_specs=hbm,
        scratch_shapes=(
            [pltpu.VMEM((span, block, wide), BF16)] * CHUNKS
            + [pltpu.VMEM((n, cap, wide), BF16)] * CHUNKS
            + [pltpu.VMEM((n, cap, wide), BF16)] * CHUNKS
            + [pltpu.VMEM((seg_dev, wide), BF16)] * CHUNKS
            + [
                pltpu.VMEM((count, width), BF16),
                pltpu.VMEM((seg_dev, width), BF16),
                pltpu.VMEM(inductance.shape, BF16),
                pltpu.VMEM((seg_dev, n * cap), BF16),
                pltpu.VMEM((n, 8, LANES), jnp.int32),
                pltpu.VMEM((n, 8, LANES), jnp.int32),
                dma((3,)),
                dma((CHUNKS + 1,)),
                dma((CHUNKS,)),
                dma((CHUNKS, n)),
                dma((CHUNKS, n)),
                dma((n,)),
                dma((n,)),
                dma((4, CHUNKS)),
                dma((4, CHUNKS)),
            ]
        ),
        compiler_params=pltpu.CompilerParams(
            collective_id=0, has_side_effects=True, vmem_limit_bytes=50 * 2**20
        ),
        cost_estimate=pl.CostEstimate(
            flops=2 * rows_dev * stored * block * block * width,
            bytes_accessed=2 * (inductance.size + 2 * base_currents.size + term_rows.size),
            transcendentals=0,
        ),
    )(block_cols, term_owner.reshape(1, count), term_slot.reshape(1, count), term_rows, base_currents, inductance)


def solution(mesh):
    placed = (
        P(("group", "row"), None),
        P(("group", "row"), None),
        P(("group", "row"), None),
        P(("group", "row"), None),
        P("row", None, None, None),
        P("row", None),
    )
    return jax.shard_map(
        shards, mesh=mesh, in_specs=placed, out_specs=P(("group", "row"), None), check_vma=False
    )
```

time: 268 us -> 93 us (0.35)
  the two profiles are of different devices: /device:TPU:12 before, /device:TPU:5 now
where the time goes in v1:
time: 93 us; the launch traced here: 92.8 us
  Pallas kernels  88.4 us (95%)
  local copies, waits for them, and re-layouts  4.4 us (5%)
    pallas_call x1, Pallas kernels, shards(): pl.pallas_call(functools.partial(kernel, n, cap), out_shape=jax.ShapeDtyp...  88.4 us
    unnamed x9, local copies, waits for them, and re-layouts  4.4 us

profile of v1, /device:TPU:5, one launch (start us, length us, event | category | flops | bytes accessed | tf_op | source)
XLA Modules:
  0.0 92.8 jit_solution(4716950726087107620)
XLA Ops:
  0.0 0.0 copy-start
  0.0 1.0 %copy-done = bf16[256,1024]{1,0:T(8,128)(2,1)S(1)} copy-done((bf16[256,1024]{1,0:T(8,128)(2,1)S(1)}, bf16[256,1024]{1,0:T(8,128)(2,1)}, u32[]{:S(2)}) %copy-start) | copy-done | bytes 524312
  1.0 0.0 copy-start.1
  1.0 0.7 copy-done.1
  1.7 0.0 copy-start.2
  1.7 0.7 copy-done.2
  2.4 0.0 copy-start.3
  2.4 0.7 copy-done.3
  3.1 88.4 %shard_map.64 = bf16[1024,1024]{1,0:T(8,128)(2,1)S(1)} custom-call(s32[4,20]{1,0:T(4,128)S(1)} %copy-done.1, s32[1,256]{1,0:T(1,128)S(1)} %bitcast.2, s32[1,256]{1,0:T(1,128)S(1)} %bitcast.3, bf16[256,1024]{1,0:T(8,128)(2,1)S(1)} %copy-done, bf16[1024,1024]{1,0:T(8,128)(2,1)} %base_hbm.1, bf16[4,20,256,256]{3,2,1,0:T(8,128)(2,1)} %blocks_hbm.1), custom_call_target="tpu_custom_call" | custom-call | flops 10737418240 | bytes 15204352 | tf_op jit(solution)/shard_map/pallas_call | solution.py:251
  91.4 1.3 %copy.8 = bf16[1024,1024]{1,0:T(8,128)(2,1)} copy(bf16[1024,1024]{1,0:T(8,128)(2,1)S(1)} %shard_map.64) | data formatting | bytes 4194304
Async XLA Ops:
  0.0 1.0 %copy-start = (bf16[256,1024]{1,0:T(8,128)(2,1)S(1)}, bf16[256,1024]{1,0:T(8,128)(2,1)}, u32[]{:S(2)}) copy-start(bf16[256,1024]{1,0:T(8,128)(2,1)} %terms_hbm.1) | copy-start | bytes 1572868
  1.0 0.7 copy-start.1
  1.7 0.7 copy-start.2
  2.4 0.7 copy-start.3

commit v2 on v1

v2 whole, which is shorter than its diff:
```python
import functools

import jax
import jax.numpy as jnp
from jax import lax
from jax.experimental import pallas as pl
from jax.experimental.pallas import tpu as pltpu
from jax.sharding import PartitionSpec as P

CHUNKS = 4
LANES = 128
HALO = 2
MESH = pl.DeviceIdType.MESH
F32 = jnp.float32
BF16 = jnp.bfloat16
TO_Y, TO_Z, TO_CORE, TO_RELAY = range(4)


def kernel(n, cap, cols_hbm, owner_hbm, slot_hbm, terms_hbm, base_hbm, blocks_hbm, out_hbm, *scratch):
    windows, scratch = scratch[:CHUNKS], scratch[CHUNKS:]
    outgoing, scratch = scratch[:CHUNKS], scratch[CHUNKS:]
    arrived, scratch = scratch[:CHUNKS], scratch[CHUNKS:]
    results, scratch = scratch[:CHUNKS], scratch[CHUNKS:]
    (cols_ref, owner_ref, slot_ref, terms, base, blocks, landing, tags_out, tags_in,
     load_sem, own_sem, store_sem, a2a_send, a2a_recv, tag_sem, halo_send, halo_recv, piece_recv) = scratch
    me = lax.axis_index("row")
    count = terms.shape[0]
    seg_dev = base.shape[0]
    rows_dev, stored, block, _ = blocks.shape
    wide = windows[0].shape[2]
    sign_c = 1 - 2 * (me % 2)
    sign_y = 1 - 2 * ((me // 2) % 2)
    z_to, z_from = me + 4 * sign_y, me - 4 * sign_y
    z_sends = jnp.logical_and(z_to >= 0, z_to < n)
    z_comes = jnp.logical_and(z_from >= 0, z_from < n)

    load_terms = pltpu.make_async_copy(terms_hbm, terms, load_sem.at[0])
    load_base = pltpu.make_async_copy(base_hbm, base, load_sem.at[1])
    load_blocks = pltpu.make_async_copy(blocks_hbm, blocks, load_sem.at[2])
    load_owner = pltpu.make_async_copy(owner_hbm, owner_ref, load_sem.at[3])
    load_slot = pltpu.make_async_copy(slot_hbm, slot_ref, load_sem.at[4])
    load_cols = pltpu.make_async_copy(cols_hbm, cols_ref, load_sem.at[5])
    for load in (load_owner, load_slot, load_terms, load_base, load_cols, load_blocks):
        load.start()

    barrier = pltpu.get_barrier_semaphore()

    @pl.loop(1, n)
    def _(step):
        pl.semaphore_signal(barrier, inc=1, device_id={"row": (me + step) % n}, device_id_type=MESH)

    load_owner.wait()
    owner = owner_ref[...]
    matches = (lax.broadcasted_iota(jnp.int32, (n, count), 0) == owner).astype(F32)
    before = lax.broadcasted_iota(jnp.int32, (count, count), 0) < lax.broadcasted_iota(jnp.int32, (count, count), 1)
    earlier = jnp.dot(matches.astype(BF16), before.astype(F32).astype(BF16), preferred_element_type=F32)
    order_in = jnp.sum(earlier * matches, axis=0, keepdims=True).astype(jnp.int32)
    position = owner * cap + order_in
    picker = (lax.broadcasted_iota(jnp.int32, (n * cap, count), 0) == position).astype(F32).astype(BF16)
    def tag_copy(peer, source):
        return pltpu.make_async_remote_copy(
            src_ref=tags_out.at[peer], dst_ref=tags_in.at[source], send_sem=tag_sem.at[0],
            recv_sem=tag_sem.at[1], device_id={"row": peer}, device_id_type=MESH)

    def row_copy(j, peer, source):
        return pltpu.make_async_remote_copy(
            src_ref=outgoing[j].at[peer], dst_ref=arrived[j].at[source], send_sem=a2a_send.at[j],
            recv_sem=a2a_recv.at[j], device_id={"row": peer}, device_id_type=MESH)

    def all_tags():
        others = pl.ds(0, n - 1)
        return pltpu.make_async_remote_copy(
            src_ref=tags_out.at[others], dst_ref=tags_in.at[others], send_sem=tag_sem.at[0],
            recv_sem=tag_sem.at[1], device_id={"row": (me + 1) % n}, device_id_type=MESH)

    def all_rows(j):
        others = pl.ds(0, n - 1)
        return pltpu.make_async_remote_copy(
            src_ref=outgoing[j].at[others], dst_ref=arrived[j].at[others], send_sem=a2a_send.at[j],
            recv_sem=a2a_recv.at[j], device_id={"row": (me + 1) % n}, device_id_type=MESH)

    own_tags = pltpu.make_async_copy(tags_out.at[me], tags_in.at[me], own_sem.at[CHUNKS])
    own_rows = [
        pltpu.make_async_copy(outgoing[j].at[me], arrived[j].at[me], own_sem.at[j]) for j in range(CHUNKS)
    ]

    def pack(j):
        sent = jnp.dot(picker, terms[:, j * wide:(j + 1) * wide], preferred_element_type=F32)
        outgoing[j][...] = sent.astype(BF16).reshape(outgoing[j].shape)

    def send_rows(j):
        @pl.loop(1, n)
        def _(step):
            row_copy(j, (me + step) % n, me).start()

        own_rows[j].start()

    load_terms.wait()
    pack(0)
    pl.semaphore_wait(barrier, n - 1)
    send_rows(0)
    per_row = LANES // cap
    lane_of = order_in + (me % per_row) * cap
    lanes = (lax.broadcasted_iota(jnp.int32, (LANES, count), 0) == lane_of).astype(F32).astype(BF16)
    load_slot.wait()
    tag = slot_ref[...] + 1
    high = (tag // 32).astype(F32)
    low = (tag % 32).astype(F32)
    over_rows = (((1,), (1,)), ((), ()))
    tags = 32.0 * lax.dot_general((matches * high).astype(BF16), lanes, over_rows, preferred_element_type=F32)
    tags = tags + lax.dot_general((matches * low).astype(BF16), lanes, over_rows, preferred_element_type=F32)
    tags = tags.astype(jnp.int32)
    for peer in range(n):
        tags_out[peer] = jnp.broadcast_to(tags[peer:peer + 1], tags_out.shape[1:])


    @pl.loop(1, n)
    def _(step):
        tag_copy((me + step) % n, me).start()

    own_tags.start()
    for j in range(1, CHUNKS):
        pack(j)
        send_rows(j)

    all_tags().wait_recv()
    own_tags.wait()
    packed = []
    for first in range(0, n, per_row):
        total = tags_in[first][0:1]
        for source in range(first + 1, min(first + per_row, n)):
            total = total + tags_in[source][0:1]
        packed.append(total)
    arrived_tags = jnp.concatenate(packed, axis=1) - 1
    tall = seg_dev // 4
    for part in range(4):
        seg_ids = lax.broadcasted_iota(jnp.int32, (tall, n * cap), 0) + part * tall
        landing[part * tall:(part + 1) * tall] = (seg_ids == arrived_tags).astype(F32).astype(BF16)
    load_base.wait()

    def halo_copy(kind, j, from_slot, to_slot, peer):
        return pltpu.make_async_remote_copy(
            src_ref=windows[j].at[pl.ds(rows_dev * from_slot, rows_dev)],
            dst_ref=windows[j].at[pl.ds(rows_dev * to_slot, rows_dev)],
            send_sem=halo_send.at[kind, j], recv_sem=halo_recv.at[kind, j],
            device_id={"row": peer}, device_id_type=MESH)

    def piece_copy(kind, p, from_slot, to_slot, peer):
        j, q = divmod(p, rows_dev)
        recv_sem = halo_recv.at[kind, j] if kind == TO_RELAY else piece_recv.at[kind, p]
        return pltpu.make_async_remote_copy(
            src_ref=windows[j].at[rows_dev * from_slot + q], dst_ref=windows[j].at[rows_dev * to_slot + q],
            send_sem=halo_send.at[kind, j], recv_sem=recv_sem, device_id={"row": peer}, device_id_type=MESH)

    y_way = (HALO, HALO - 2 * sign_y, me + 2 * sign_y)
    core_way = (HALO, HALO - sign_c, me + sign_c)
    z_way = (HALO + 2 * sign_y, HALO - 2 * sign_y, z_to)
    relay_way = (HALO + 2 * sign_c, HALO + sign_c, me + sign_c)
    relay_sends = jnp.logical_or(sign_y == sign_c, z_comes)
    relay_comes = jnp.logical_or(sign_y != sign_c, z_comes)
    first_block = (me - HALO) * rows_dev
    pieces = CHUNKS * rows_dev

    def own(j):
        all_rows(j).wait_recv()
        own_rows[j].wait()
        rows = arrived[j][...].reshape(n * cap, wide)
        for q in range(rows_dev):
            place = slice(q * block, (q + 1) * block)
            injected = jnp.dot(landing[place], rows, preferred_element_type=F32)
            before_it = base[place, j * wide:(j + 1) * wide].astype(F32)
            windows[j][HALO * rows_dev + q] = (before_it + injected).astype(BF16)
            piece_copy(TO_Y, j * rows_dev + q, *y_way).start()
        halo_copy(TO_CORE, j, *core_way).start()

    def y_arrives(p):
        slot = HALO + 2 * sign_y
        piece_copy(TO_Y, p, slot, slot, me + 2 * sign_y).wait_recv()

        @pl.when(z_sends)
        def _():
            piece_copy(TO_Z, p, *z_way).start()

        @pl.when(sign_y == sign_c)
        def _():
            piece_copy(TO_RELAY, p, *relay_way).start()

    def z_arrives(p):
        slot = HALO - 2 * sign_y

        @pl.when(z_comes)
        def _():
            piece_copy(TO_Z, p, slot, slot, me + 2 * sign_y).wait_recv()

        @pl.when(jnp.logical_and(z_comes, sign_y != sign_c))
        def _():
            piece_copy(TO_RELAY, p, *relay_way).start()

    def window_complete(j):
        halo_copy(TO_CORE, j, HALO + sign_c, HALO + sign_c, me + sign_c).wait_recv()

        @pl.when(relay_comes)
        def _():
            halo_copy(TO_RELAY, j, HALO - sign_c, HALO - sign_c, me + sign_c).wait_recv()

    def compute(j, r):
        total = jnp.zeros((block, wide), F32)
        for k in range(stored):
            place = jnp.clip(cols_ref[r, k] - first_block, 0, windows[j].shape[0] - 1)
            total = total + jnp.dot(blocks[r, k], windows[j][place], preferred_element_type=F32)
        results[j][r * block:(r + 1) * block] = total.astype(BF16)

    def store(j):
        return pltpu.make_async_copy(results[j], out_hbm.at[:, pl.ds(j * wide, wide)], store_sem.at[j])

    own(0)
    own(1)
    z_lag, lag = 2, rows_dev + 2
    for p in range(pieces + lag):
        if p < pieces:
            y_arrives(p)
            if p % rows_dev == 0 and p // rows_dev + 2 < CHUNKS:
                own(p // rows_dev + 2)
        if 0 <= p - z_lag < pieces:
            z_arrives(p - z_lag)
        if p == lag:
            load_cols.wait()
            load_blocks.wait()
            all_tags().wait_send()
            for j in range(CHUNKS):
                all_rows(j).wait_send()
        if p >= lag:
            j, r = divmod(p - lag, rows_dev)
            if r == 0:
                window_complete(j)
            compute(j, r)
            if r == rows_dev - 1:
                store(j).start()

    for j in range(CHUNKS):
        halo_copy(TO_Y, j, *y_way).wait_send()
        halo_copy(TO_CORE, j, *core_way).wait_send()

        @pl.when(z_sends)
        def _():
            halo_copy(TO_Z, j, *z_way).wait_send()

        @pl.when(relay_sends)
        def _():
            halo_copy(TO_RELAY, j, *relay_way).wait_send()

        store(j).wait()


def shards(base_currents, term_rows, term_owner, term_slot, inductance, block_cols):
    n = lax.axis_size("row")
    seg_dev, width = base_currents.shape
    count = term_rows.shape[0]
    rows_dev, stored, block, _ = inductance.shape
    cap = max(16, 2 * count // n)
    wide = width // CHUNKS
    span = (2 * HALO + 1) * rows_dev
    hbm = pl.BlockSpec(memory_space=pl.ANY)
    dma = pltpu.SemaphoreType.DMA
    return pl.pallas_call(
        functools.partial(kernel, n, cap),
        out_shape=jax.ShapeDtypeStruct((seg_dev, width), BF16),
        in_specs=[hbm] * 6,
        out_specs=hbm,
        scratch_shapes=(
            [pltpu.VMEM((span, block, wide), BF16)] * CHUNKS
            + [pltpu.VMEM((n, cap, wide), BF16)] * CHUNKS
            + [pltpu.VMEM((n, cap, wide), BF16)] * CHUNKS
            + [pltpu.VMEM((seg_dev, wide), BF16)] * CHUNKS
            + [
                pltpu.SMEM(block_cols.shape, jnp.int32),
                pltpu.VMEM((1, count), jnp.int32),
                pltpu.VMEM((1, count), jnp.int32),
                pltpu.VMEM((count, width), BF16),
                pltpu.VMEM((seg_dev, width), BF16),
                pltpu.VMEM(inductance.shape, BF16),
                pltpu.VMEM((seg_dev, n * cap), BF16),
                pltpu.VMEM((n, 8, LANES), jnp.int32),
                pltpu.VMEM((n, 8, LANES), jnp.int32),
                dma((6,)),
                dma((CHUNKS + 1,)),
                dma((CHUNKS,)),
                dma((CHUNKS,)),
                dma((CHUNKS,)),
                dma((2,)),
                dma((4, CHUNKS)),
                dma((4, CHUNKS)),
                dma((2, CHUNKS * rows_dev)),
            ]
        ),
        compiler_params=pltpu.CompilerParams(
            collective_id=0, has_side_effects=True, vmem_limit_bytes=60 * 2**20
        ),
        cost_estimate=pl.CostEstimate(
            flops=2 * rows_dev * stored * block * block * width,
            bytes_accessed=2 * (inductance.size + 2 * base_currents.size + term_rows.size),
            transcendentals=0,
        ),
    )(block_cols, term_owner.reshape(1, count), term_slot.reshape(1, count), term_rows, base_currents, inductance)


def solution(mesh):
    placed = (
        P(("group", "row"), None),
        P(("group", "row"), None),
        P(("group", "row"), None),
        P(("group", "row"), None),
        P("row", None, None, None),
        P("row", None),
    )
    return jax.shard_map(
        shards, mesh=mesh, in_specs=placed, out_specs=P(("group", "row"), None), check_vma=False
    )
```

time: 93 us -> 83.1 us (0.89)
  Pallas kernels: 88.4 us -> 79.1 us
  local copies, waits for them, and re-layouts: 4.4 us -> 3.08 us
    pallas_call x1, Pallas kernels: 88.4 us -> 79.1 us  [shards(): pl.pallas_call(functools.partial(kernel, n, cap), out_shape=jax.ShapeDtyp...]
    unnamed x9 -> x1, local copies, waits for them, and re-layouts: 4.4 us -> 3.08 us
where the time goes in v2:
time: 83.1 us; the launch traced here: 82.2 us
  Pallas kernels  79.1 us (95%)
  local copies, waits for them, and re-layouts  3.08 us (4%)
    pallas_call x1, Pallas kernels, shards(): pl.pallas_call(functools.partial(kernel, n, cap), out_shape=jax.ShapeDtyp...  79.1 us
    unnamed x1, local copies, waits for them, and re-layouts  3.08 us

profile of v2, /device:TPU:5, one launch (start us, length us, event | category | flops | bytes accessed | tf_op | source)
XLA Modules:
  0.0 82.2 jit_solution(16680132946076764218)
XLA Ops:
  0.0 79.1 %shard_map.64 = bf16[1024,1024]{1,0:T(8,128)(2,1)} custom-call(s32[4,20]{1,0:T(4,128)} %cols_hbm.1, s32[1,256]{1,0:T(1,128)} %bitcast.2, s32[1,256]{1,0:T(1,128)} %bitcast.3, bf16[256,1024]{1,0:T(8,128)(2,1)} %terms_hbm.1, bf16[1024,1024]{1,0:T(8,128)(2,1)} %base_hbm.1, bf16[4,20,256,256]{3,2,1,0:T(8,128)(2,1)} %blocks_hbm.1), custom_call_target="tpu_custom_call" | custom-call | flops 10737418240 | bytes 15204352 | tf_op jit(solution)/shard_map/pallas_call | solution.py:265
  79.1 3.1 %copy.8 = bf16[1024,1024]{1,0:T(8,128)(2,1)} copy(bf16[1024,1024]{1,0:T(8,128)(2,1)} %shard_map.64) | data formatting | bytes 4194304

commit v3 on v2

--- a/solution.py
+++ b/solution.py
@@ -119,9 +119,13 @@
         tag_copy((me + step) % n, me).start()
 
     own_tags.start()
-    for j in range(1, CHUNKS):
+
+    def next_rows(j):
         pack(j)
+        all_rows(j - 1).wait_send()
         send_rows(j)
+
+    next_rows(1)
 
     all_tags().wait_recv()
     own_tags.wait()
@@ -213,8 +217,10 @@
     def store(j):
         return pltpu.make_async_copy(results[j], out_hbm.at[:, pl.ds(j * wide, wide)], store_sem.at[j])
 
-    own(0)
-    own(1)
+    for j in range(CHUNKS - 2):
+        if j < 2:
+            own(j)
+        next_rows(j + 2)
     z_lag, lag = 2, rows_dev + 2
     for p in range(pieces + lag):
         if p < pieces:
@@ -227,8 +233,7 @@
             load_cols.wait()
             load_blocks.wait()
             all_tags().wait_send()
-            for j in range(CHUNKS):
-                all_rows(j).wait_send()
+            all_rows(CHUNKS - 1).wait_send()
         if p >= lag:
             j, r = divmod(p - lag, rows_dev)
             if r == 0:

time: 83.1 us -> 91.5 us (1.10)
  Pallas kernels: 79.1 us -> 86.7 us
    pallas_call x1, Pallas kernels: 79.1 us -> 86.7 us  [shards(): pl.pallas_call(functools.partial(kernel, n, cap), out_shape=jax.ShapeDtyp...]
where the time goes in v3:
time: 91.5 us; the launch traced here: 89.8 us
  Pallas kernels  86.7 us (95%)
  local copies, waits for them, and re-layouts  3.08 us (3%)
    pallas_call x1, Pallas kernels, shards(): pl.pallas_call(functools.partial(kernel, n, cap), out_shape=jax.ShapeDtyp...  86.7 us
    unnamed x1, local copies, waits for them, and re-layouts  3.08 us

profile of v3, /device:TPU:5, one launch (start us, length us, event | category | flops | bytes accessed | tf_op | source)
XLA Modules:
  0.0 89.8 jit_solution(5940687782558840783)
XLA Ops:
  0.0 86.7 %shard_map.64 = bf16[1024,1024]{1,0:T(8,128)(2,1)} custom-call(s32[4,20]{1,0:T(4,128)} %cols_hbm.1, s32[1,256]{1,0:T(1,128)} %bitcast.2, s32[1,256]{1,0:T(1,128)} %bitcast.3, bf16[256,1024]{1,0:T(8,128)(2,1)} %terms_hbm.1, bf16[1024,1024]{1,0:T(8,128)(2,1)} %base_hbm.1, bf16[4,20,256,256]{3,2,1,0:T(8,128)(2,1)} %blocks_hbm.1), custom_call_target="tpu_custom_call" | custom-call | flops 10737418240 | bytes 15204352 | tf_op jit(solution)/shard_map/pallas_call | solution.py:270
  86.7 3.1 %copy.8 = bf16[1024,1024]{1,0:T(8,128)(2,1)} copy(bf16[1024,1024]{1,0:T(8,128)(2,1)} %shard_map.64) | data formatting | bytes 4194304
